TPU v7x, 32 devices: a whole 2x2x4 slice. The times are simulated.
32 devices in a mesh: section: 2 (over core), group: 4 (over z), rep: 4 (over y, x).
Axes of the slice: x: 2, y: 2, z: 4, core: 2. Of those that a mesh axis runs over, the one named last changes fastest.
Arguments:
- latents: bfloat16 [32, 256, 384], P(('group', 'rep')), may hold values from -6 to 6
- cond: float32 [32, 384], P(('group', 'rep')), may hold values from -6 to 6
- cotangent: bfloat16 [32, 256, 384], P(('group', 'rep')), may hold values from -6 to 6
- live_count: int32 [16, 2], P(('group', 'rep')), may hold values from 0 to 1, as said below
- adaptive_weight: bfloat16 [2, 384, 2304], P('section', 'group'), may hold values from -0.3125 to 0.3125
- adaptive_bias: bfloat16 [2, 2304], P('section', 'group'), may hold values from 0.5 to 1.5
- query_key_value_weight: bfloat16 [2, 384, 1152], P('section', 'group'), may hold values from -0.15625 to 0.15625
- output_projection_weight: bfloat16 [2, 384, 384], P('section', 'group'), may hold values from -1.25 to 1.25
- first_dense_weight: bfloat16 [2, 384, 1536], P('section', 'group'), may hold values from -0.3125 to 0.3125
- first_dense_bias: bfloat16 [2, 1536], P('section', 'group'), may hold values from -3 to 3
- second_dense_weight: bfloat16 [2, 1536, 384], P('section', 'group'), may hold values from -0.15625 to 0.15625
Outputs:
- section_outputs: bfloat16 [2, 32, 256, 384], P('section', ('group', 'rep'))
- input_grads: float32 [2, 32, 256, 384], P('section', ('group', 'rep'))
- cond_grads: float32 [2, 32, 384], P('section', ('group', 'rep'))
- grad_ada: float32 [2, 384, 2304], P('section', 'group')
- grad_bada: float32 [2, 2304], P('section', 'group')
- grad_qkv: float32 [2, 384, 1152], P('section', 'group')
- grad_proj: float32 [2, 384, 384], P('section', 'group')
- grad_fc1: float32 [2, 384, 1536], P('section', 'group')
- grad_bfc1: float32 [2, 1536], P('section', 'group')
- grad_fc2: float32 [2, 1536, 384], P('section', 'group')
Inputs may be any that keep to these rules, and one draw needn't show every extreme that they name: live_count of a device block and micro-batch counts the real latents, which fill its first slots; the rest hold no latent. In every micro-batch one device block has 1 and another has none.
All inputs are finite; a program needn't handle non-finite values.
Results may differ from a plain program's by a relative error of at most 0.018.
Values may be sent and summed in bfloat16 or wider, within the bound.
A program may use at most 192 MiB of HBM per device.

v0:
```python
from functools import partial
import jax
import jax.numpy as jnp
from jax import lax
from jax.sharding import PartitionSpec as P

D = 384
HEADS = 6
HEAD_DIM = 64
FF = 1536
TOK = 256
MB = 2
SLOTS = 1
epsilon = 1e-06


def passed_along(value, axis, steps):
    count = lax.axis_size(axis)
    first, last = (max(0, -steps), min(count, count - steps))
    return lax.ppermute(value, axis, [(source, source + steps) for source in range(first, last)])


def for_sending(x):
    return jax.tree.map(lambda a: a.astype(jnp.bfloat16) if a.dtype == jnp.float32 else a, x)


def normalize(values):
    center = values - jnp.mean(values, axis=-1, keepdims=True)
    spread = jnp.mean(center * center, axis=-1, keepdims=True)
    return center * lax.rsqrt(spread + epsilon)


def modulate(values, scale_part, shift_part):
    return normalize(values) * (1.0 + scale_part[:, None, :]) + shift_part[:, None, :]


def heads_of(array, offset):
    count, length = (array.shape[0], array.shape[1])
    return array[..., offset * D : (offset + 1) * D].reshape(count, length, HEADS, HEAD_DIM)


def attention_scores(queries, keys_part):
    scores = jnp.einsum("snhe,smhe->shnm", queries, keys_part, preferred_element_type=jnp.float32)
    return scores * HEAD_DIM ** (-0.5)


def forward_block(input_rows, condition_vector, weights):
    (
        adaptive_weight,
        adaptive_bias,
        query_key_value_weight,
        output_projection_weight,
        first_dense_weight,
        first_dense_bias,
        second_dense_weight,
    ) = weights
    silu_low = jax.nn.silu(condition_vector).astype(jnp.bfloat16)
    modulation = jnp.dot(
        silu_low, adaptive_weight, preferred_element_type=jnp.float32
    ) + adaptive_bias.astype(jnp.float32)
    shift_attn, scale_attn, gate_attn, shift_mlp, scale_mlp, gate_mlp = jnp.split(
        modulation, 6, axis=-1
    )
    widened = input_rows.astype(jnp.float32)
    normed_reduced = modulate(widened, scale_attn, shift_attn).astype(jnp.bfloat16)
    triple_low = jnp.dot(
        normed_reduced, query_key_value_weight, preferred_element_type=jnp.float32
    ).astype(jnp.bfloat16)
    queries = heads_of(triple_low, 0)
    keys_part = heads_of(triple_low, 1)
    values_part = heads_of(triple_low, 2)
    scores = attention_scores(queries, keys_part)
    highest = jnp.max(scores, axis=-1, keepdims=True)
    log_total = highest + jnp.log(jnp.sum(jnp.exp(scores - highest), axis=-1, keepdims=True))
    probs_low = jnp.exp(scores - log_total).astype(jnp.bfloat16)
    mixed = jnp.einsum(
        "shnm,smhe->snhe", probs_low, values_part, preferred_element_type=jnp.float32
    )
    mixed_reduced = mixed.reshape(input_rows.shape).astype(jnp.bfloat16)
    attended = jnp.dot(mixed_reduced, output_projection_weight, preferred_element_type=jnp.float32)
    middle = widened + gate_attn[:, None, :] * attended
    second_low = modulate(middle, scale_mlp, shift_mlp).astype(jnp.bfloat16)
    hidden = jnp.dot(
        second_low, first_dense_weight, preferred_element_type=jnp.float32
    ) + first_dense_bias.astype(jnp.float32)
    active_low = jax.nn.gelu(hidden, approximate=True).astype(jnp.bfloat16)
    branch = jnp.dot(active_low, second_dense_weight, preferred_element_type=jnp.float32)
    result = middle + gate_mlp[:, None, :] * branch
    kept_state = (
        input_rows,
        condition_vector,
        modulation,
        normed_reduced,
        triple_low,
        log_total[..., 0],
        mixed_reduced,
        attended,
        middle,
        second_low,
        hidden,
        active_low,
        branch,
    )
    return (result, kept_state)


def forward_empty(input_rows, condition_vector, weights):
    count, length = (input_rows.shape[0], input_rows.shape[1])
    rows_float = jnp.zeros((count, length, D), jnp.float32)
    rows_low = jnp.zeros((count, length, D), jnp.bfloat16)
    kept_state = (
        rows_low,
        jnp.zeros((count, D), jnp.float32),
        jnp.zeros((count, 6 * D), jnp.float32),
        rows_low,
        jnp.zeros((count, length, 3 * D), jnp.bfloat16),
        jnp.zeros((count, HEADS, length), jnp.float32),
        rows_low,
        rows_float,
        rows_float,
        rows_low,
        jnp.zeros((count, length, FF), jnp.float32),
        jnp.zeros((count, length, FF), jnp.bfloat16),
        rows_float,
    )
    return (rows_float, kept_state)


def backward_block(out_grad, kept_state, weights):
    (
        adaptive_weight,
        adaptive_bias,
        query_key_value_weight,
        output_projection_weight,
        first_dense_weight,
        first_dense_bias,
        second_dense_weight,
    ) = weights
    (
        input_rows,
        condition_vector,
        modulation,
        normed_reduced,
        triple_low,
        log_total,
        mixed_reduced,
        attended,
        middle,
        second_low,
        hidden,
        active_low,
        branch,
    ) = kept_state
    count, length = (input_rows.shape[0], input_rows.shape[1])
    shift_attn, scale_attn, gate_attn, shift_mlp, scale_mlp, gate_mlp = jnp.split(
        modulation, 6, axis=-1
    )
    grad_gate_mlp = jnp.sum(out_grad * branch, axis=1)
    branch_low = (gate_mlp[:, None, :] * out_grad).astype(jnp.bfloat16)
    grad_fc2 = jnp.einsum("snf,snd->fd", active_low, branch_low, preferred_element_type=jnp.float32)
    grad_active = jnp.einsum(
        "snd,fd->snf", branch_low, second_dense_weight, preferred_element_type=jnp.float32
    )
    unused, gelu_back = jax.vjp(partial(jax.nn.gelu, approximate=True), hidden)
    hidden_low = gelu_back(grad_active)[0].astype(jnp.bfloat16)
    grad_bias = jnp.sum(hidden_low, axis=(0, 1), dtype=jnp.float32)
    grad_fc1 = jnp.einsum("snd,snf->df", second_low, hidden_low, preferred_element_type=jnp.float32)
    grad_second = jnp.einsum(
        "snf,df->snd", hidden_low, first_dense_weight, preferred_element_type=jnp.float32
    )
    unused, norm_back = jax.vjp(modulate, middle, scale_mlp, shift_mlp)
    grad_middle, grad_scale_mlp, grad_shift_mlp = norm_back(grad_second)
    grad_middle = grad_middle + out_grad
    grad_gate_attn = jnp.sum(grad_middle * attended, axis=1)
    attended_reduced = (gate_attn[:, None, :] * grad_middle).astype(jnp.bfloat16)
    grad_proj = jnp.einsum(
        "row,rol->wl", mixed_reduced, attended_reduced, preferred_element_type=jnp.float32
    )
    mixed_grad_low = jnp.einsum(
        "lqa,ia->lqi",
        attended_reduced,
        output_projection_weight,
        preferred_element_type=jnp.float32,
    ).astype(jnp.bfloat16)
    heads_grad = mixed_grad_low.reshape(count, length, HEADS, HEAD_DIM)
    queries = heads_of(triple_low, 0)
    keys_part = heads_of(triple_low, 1)
    values_part = heads_of(triple_low, 2)
    probs = jnp.exp(attention_scores(queries, keys_part) - log_total[..., None])
    probs_low = probs.astype(jnp.bfloat16)
    grad_values = jnp.einsum(
        "shnm,snhe->smhe", probs_low, heads_grad, preferred_element_type=jnp.float32
    )
    grad_probs = jnp.einsum(
        "snhe,smhe->shnm", heads_grad, values_part, preferred_element_type=jnp.float32
    )
    scores_low = (
        probs * (grad_probs - jnp.sum(grad_probs * probs, axis=-1, keepdims=True))
    ).astype(jnp.bfloat16)
    grad_queries = jnp.einsum(
        "shnm,smhe->snhe", scores_low, keys_part, preferred_element_type=jnp.float32
    ) * HEAD_DIM ** (-0.5)
    grad_keys = jnp.einsum(
        "shnm,snhe->smhe", scores_low, queries, preferred_element_type=jnp.float32
    ) * HEAD_DIM ** (-0.5)
    triple_gradient_reduced = jnp.concatenate(
        [
            grad_queries.reshape(count, length, D),
            grad_keys.reshape(count, length, D),
            grad_values.reshape(count, length, D),
        ],
        axis=-1,
    ).astype(jnp.bfloat16)
    grad_qkv = jnp.einsum(
        "row,rol->wl", normed_reduced, triple_gradient_reduced, preferred_element_type=jnp.float32
    )
    grad_normed = jnp.einsum(
        "lqa,ia->lqi",
        triple_gradient_reduced,
        query_key_value_weight,
        preferred_element_type=jnp.float32,
    )
    unused, first_back = jax.vjp(modulate, input_rows.astype(jnp.float32), scale_attn, shift_attn)
    grad_inputs, grad_scale_attn, grad_shift_attn = first_back(grad_normed)
    grad_inputs = grad_inputs + grad_middle
    modulation_low = jnp.concatenate(
        [
            grad_shift_attn,
            grad_scale_attn,
            grad_gate_attn,
            grad_shift_mlp,
            grad_scale_mlp,
            grad_gate_mlp,
        ],
        axis=-1,
    ).astype(jnp.bfloat16)
    grad_bada = jnp.sum(modulation_low, axis=0, dtype=jnp.float32)
    silu_low = jax.nn.silu(condition_vector).astype(jnp.bfloat16)
    grad_ada = jnp.dot(silu_low.T, modulation_low, preferred_element_type=jnp.float32)
    grad_silu = jnp.dot(modulation_low, adaptive_weight.T, preferred_element_type=jnp.float32)
    unused, silu_back = jax.vjp(jax.nn.silu, condition_vector)
    grad_condition = silu_back(grad_silu)[0]
    return (
        grad_inputs,
        grad_condition,
        (grad_ada, grad_bada, grad_qkv, grad_proj, grad_fc1, grad_bias, grad_fc2),
    )


def backward_empty(out_grad, kept_state, weights):
    count = out_grad.shape[0]
    grads = tuple((jnp.zeros(array.shape, jnp.float32) for array in weights))
    return (jnp.zeros(out_grad.shape, jnp.float32), jnp.zeros((count, D), jnp.float32), grads)


def stripped(gathered):
    return tuple((array[0] for array in gathered))


def body(
    latents,
    cond,
    cotangent,
    live_count,
    adaptive_weight,
    adaptive_bias,
    query_key_value_weight,
    output_projection_weight,
    first_dense_weight,
    first_dense_bias,
    second_dense_weight,
):
    is_first = lax.axis_index("section") == 0
    inputs_all = latents.reshape(MB, SLOTS, TOK, D)
    conds_all = cond.reshape(MB, SLOTS, D)
    tangents_all = cotangent.reshape(MB, SLOTS, TOK, D)
    live = (jnp.arange(SLOTS, dtype=jnp.int32)[None, :] < live_count[0][:, None]).astype(
        jnp.float32
    )
    kept_weights = stripped(
        (
            lax.all_gather(adaptive_weight, "group", axis=1, tiled=True),
            lax.all_gather(adaptive_bias, "group", axis=1, tiled=True),
            lax.all_gather(query_key_value_weight, "group", axis=1, tiled=True),
            lax.all_gather(output_projection_weight, "group", axis=1, tiled=True),
            lax.all_gather(first_dense_weight, "group", axis=1, tiled=True),
            lax.all_gather(first_dense_bias, "group", axis=1, tiled=True),
            lax.all_gather(second_dense_weight, "group", axis=1, tiled=True),
        )
    )
    received = jnp.zeros((SLOTS, TOK, D), jnp.bfloat16)
    forward_out = []
    states = []
    for moment in range(MB + 1):
        weights = kept_weights
        own_rows = inputs_all[min(moment, MB - 1)]
        rows_in = jnp.where(is_first, own_rows, received)
        cond_in = jnp.where(is_first, conds_all[min(moment, MB - 1)], conds_all[max(moment - 1, 0)])
        active = jnp.where(is_first, moment < MB, moment >= 1)
        result, kept_state = lax.cond(
            active, forward_block, forward_empty, rows_in, cond_in, weights
        )
        result_low = result.astype(jnp.bfloat16)
        forward_out.append(result_low)
        states.append(kept_state)
        if moment < MB:
            received = passed_along(result_low, "section", 1)
    grad_recv = jnp.zeros((SLOTS, TOK, D), jnp.bfloat16)
    cond_recv = jnp.zeros((SLOTS, D), jnp.bfloat16)
    backward_out = []
    owned = None
    totals = None
    for moment in range(MB + 1):
        weights = kept_weights
        earlier = max(MB - 1 - moment, 0)
        out_grad = jnp.where(
            is_first,
            grad_recv.astype(jnp.float32),
            tangents_all[earlier].astype(jnp.float32) * live[earlier][:, None, None],
        )
        kept_state = states[MB - moment]
        active = jnp.where(is_first, moment >= 1, moment < MB)
        grad_rows, grad_cond, grads = lax.cond(
            active, backward_block, backward_empty, out_grad, kept_state, weights
        )
        rows_low = grad_rows.astype(jnp.bfloat16)
        cond_low = grad_cond.astype(jnp.bfloat16)
        backward_out.append((grad_rows, grad_cond, rows_low, cond_low, cond_recv))
        totals = (
            grads
            if totals is None
            else jax.tree.map(lambda former, latter: former + latter, totals, grads)
        )
        if moment < MB:
            grad_recv, cond_recv = passed_along((rows_low, cond_low), "section", -1)
    owned = jax.tree.map(
        lambda part: part.astype(jnp.float32),
        lax.psum_scatter(for_sending(totals), "group", scatter_dimension=0, tiled=True),
    )
    owned = jax.tree.map(lambda part: part.astype(jnp.float32), lax.psum(for_sending(owned), "rep"))
    outputs_list = []
    input_list = []
    cond_list = []
    for batch in range(MB):
        alive = live[batch].astype(jnp.bfloat16)[:, None, None]
        outputs_list.append(jnp.where(is_first, forward_out[batch], forward_out[batch + 1]) * alive)
        early = backward_out[MB - batch]
        late = backward_out[MB - 1 - batch]
        input_list.append(jnp.where(is_first, early[0], late[2].astype(jnp.float32)))
        cond_list.append(
            jnp.where(
                is_first, early[1] + early[4].astype(jnp.float32), late[3].astype(jnp.float32)
            )
        )
    section_outputs = jnp.concatenate(outputs_list, axis=0)[None]
    input_grads = jnp.concatenate(input_list, axis=0)[None]
    cond_grads = jnp.concatenate(cond_list, axis=0)[None]
    return (
        section_outputs,
        input_grads,
        cond_grads,
        owned[0][None],
        owned[1][None],
        owned[2][None],
        owned[3][None],
        owned[4][None],
        owned[5][None],
        owned[6][None],
    )


def solution(mesh):
    return jax.shard_map(
        body,
        mesh=mesh,
        in_specs=(
            P(("group", "rep"), None, None),
            P(("group", "rep"), None),
            P(("group", "rep"), None, None),
            P(("group", "rep"), None),
            P("section", "group", None),
            P("section", "group"),
            P("section", "group", None),
            P("section", "group", None),
            P("section", "group", None),
            P("section", "group"),
            P("section", "group", None),
        ),
        out_specs=(
            P("section", ("group", "rep"), None, None),
            P("section", ("group", "rep"), None, None),
            P("section", ("group", "rep"), None),
            P("section", "group", None),
            P("section", "group"),
            P("section", "group", None),
            P("section", "group", None),
            P("section", "group", None),
            P("section", "group"),
            P("section", "group", None),
        ),
        check_vma=False,
    )
```

profile of v0, /device:TPU:0, one launch (start us, length us, event | category | flops | bytes accessed | tf_op | source)
XLA Modules:
  0.0 573.9 jit_solution(1712281635695127555)
XLA Ops:
  12.1 13.8 %all_gather.26 = bf16[1,1536]{1,0:T(2,128)(2,1)S(1)} all-gather(bf16[1,384]{1,0:T(2,128)(2,1)} %param.28), channel_id=1, replica_groups=mesh['section'=2,'group'=4,'rep'=4] {'group'}, dimensions={1}, use_global_device_ids=true | all-gather | bytes 3840 | tf_op jit(solution)/shard_map/all_gather | solution.py:287
  30.5 11.2 %all-reduce = bf16[2304]{0:T(1024)(128)(2,1)S(1)} all-reduce(bf16[2304]{0:T(1024)(128)(2,1)S(1)} %dynamic-update-slice), channel_id=1, replica_groups=mesh['section'=2,'group'=4,'rep'=4] {'group'}, use_global_device_ids=true, to_apply=%add | all-reduce | flops 2304 | bytes 9216 | tf_op jit(solution)/shard_map/squeeze | solution.py:257
  41.6 14.0 %all_gather.24 = bf16[1,384,384]{2,1,0:T(8,128)(2,1)S(1)} all-gather(bf16[1,96,384]{2,1,0:T(8,128)(2,1)S(1)} %copy-done.114), channel_id=1, replica_groups=mesh['section'=2,'group'=4,'rep'=4] {'group'}, dimensions={1}, use_global_device_ids=true | all-gather | bytes 368640 | tf_op jit(solution)/shard_map/all_gather | solution.py:285
  57.5 31.4 %all_gather.23 = bf16[1,384,1152]{2,1,0:T(8,128)(2,1)S(1)} all-gather(bf16[1,96,1152]{2,1,0:T(8,128)(2,1)S(1)} %copy-done.102), channel_id=1, replica_groups=mesh['section'=2,'group'=4,'rep'=4] {'group'}, dimensions={1}, use_global_device_ids=true | all-gather | bytes 1105920 | tf_op jit(solution)/shard_map/all_gather | solution.py:284
  88.9 41.7 %all-gather.4.cloned.1.call-done = bf16[1,384,2304]{2,1,0:T(8,128)(2,1)} async-done(((bf16[1,96,2304]{2,1,0:T(8,128)(2,1)}), bf16[1,384,2304]{2,1,0:T(8,128)(2,1)}) %all-gather.4.cloned.1.call-update) | async-done | bytes 1769488 | tf_op jit(solution)/shard_map/all_gather | solution.py:282
  130.6 13.2 %conditional.4 = (bf16[1,256,384]{2,1,0:T(8,128)(2,1)S(1)}, f32[1,384]{1,0:T(1,128)}, f32[1,2304]{1,0:T(1,128)S(1)}, bf16[1,256,384]{2,1,0:T(8,128)(2,1)}, bf16[...) conditional(s32[]{:T(128)} %convert_element_type.491, () %tuple.65, ...), branch_computations={%region_0.1_spmd, %region_1.8_spmd} | conditional | flops 1021386368 | bytes 41346496 | solution.py:300
  130.6 1.8 convolution_reduce_fusion
  137.2 1.7 convolution_add_fusion
  138.9 2.8 fusion.16
  141.8 1.9 fusion.29
  145.8 1.8 convolution_reduce_fusion.2
  157.7 10.2 %conditional.5 = (bf16[1,256,384]{2,1,0:T(8,128)(2,1)S(1)}, f32[1,384]{1,0:T(1,128)}, f32[1,2304]{1,0:T(1,128)}, bf16[1,256,384]{2,1,0:T(8,128)(2,1)}, bf16[1,25...) conditional(s32[]{:T(128)} %convert_element_type.509, () %tuple.67, ...), branch_computations={%region_14.15_spmd, %region_15.22_spmd} | conditional | flops 1021386368 | bytes 41874824 | solution.py:300
  167.9 9.5 %conditional.6 = (f32[384,2304]{1,0:T(8,128)}, f32[2304]{0:T(1024)S(1)}, f32[1536]{0:T(1024)S(1)}, bf16[1,256,384]{2,1,0:T(8,128)(2,1)S(1)}, bf16[1,384]{1,0:T(2...) conditional(s32[]{:T(128)} %convert_element_type.509, () %tuple.70, ...), branch_computations={%region_22.23_spmd, %region_23.40_spmd} | conditional | flops 2089162752 | bytes 87958680 | solution.py:323
  173.6 1.7 broadcast.903.clone
  175.4 2.0 broadcast.899
  178.9 92.8 %collective-permute-done.2 = bf16[1,256,384]{2,1,0:T(8,128)(2,1)S(1)} collective-permute-done((bf16[1,256,384]{2,1,0:T(8,128)(2,1)S(1)}, bf16[1,256,384]{2,1,0:T(8,128)(2,1)S(1)}, u32[]{:S(2)}, u32[]{:S(2)}) %collective-permute-start.2) | collective-permute-done | bytes 196640 | tf_op jit(solution)/shard_map/ppermute | solution.py:20
  271.8 4.6 convert_reduce_fusion.8
  278.4 2.1 fusion.169
  282.3 1.8 copy.127
  291.7 2.0 collective-permute-done.3
  294.6 58.3 %conditional.7 = (f32[1,256,384]{2,1,0:T(8,128)}, f32[1,384]{1,0:T(1,128)}, f32[384,2304]{1,0:T(8,128)}, f32[2304]{0:T(1024)}, f32[1536]{0:T(1024)}, /*index=5*/...) conditional(s32[]{:T(128)} %convert_element_type.491, () %tuple.69, ...), branch_computations={%region_45.46_spmd, %region_46.63_spmd} | conditional | flops 2088473856 | bytes 92844544 | solution.py:323
  298.3 2.0 convert_reduce_fusion.7
  300.2 1.8 multiply_reduce_fusion.7
  302.1 3.6 convert_reduce_fusion.5
  311.3 1.9 multiply_reduce_fusion.8
  317.3 2.1 convolution_bitcast_fusion.9
  319.4 2.1 copy.164
  321.5 2.1 copy.131
  332.1 2.0 add_add_fusion.5
  336.5 1.9 copy.162
  338.4 3.3 convolution_bitcast_fusion.5
  341.7 3.2 copy.168
  344.9 2.0 convolution_bitcast_fusion.6
  346.9 3.2 copy.166
  350.1 2.9 broadcast_multiply_fusion.7
  352.9 2.3 add_convert_fusion.7
  355.4 3.7 add_convert_fusion.6
  359.5 4.1 add_convert_fusion.5
  363.7 5.7 add_convert_fusion.4
  371.8 4.9 add_convert_fusion.3
  381.1 18.7 %reduce-scatter.8.cloned.1.call-done = bf16[96,1152]{1,0:T(8,128)(2,1)} async-done(((bf16[384,1152]{1,0:T(8,128)(2,1)}), bf16[96,1152]{1,0:T(8,128)(2,1)}) %reduce-scatter.8.cloned.1.call-update) | async-done | bytes 221200 | tf_op jit(solution)/shard_map/reduce_scatter | solution.py:338
  399.8 30.4 %reduce-scatter.12.cloned.1.call-done = bf16[96,1536]{1,0:T(8,128)(2,1)} async-done(((bf16[384,1536]{1,0:T(8,128)(2,1)}), bf16[96,1536]{1,0:T(8,128)(2,1)}) %reduce-scatter.12.cloned.1.call-update) | async-done | bytes 294928 | tf_op jit(solution)/shard_map/reduce_scatter | solution.py:338
  430.2 30.2 %reduce-scatter.14.cloned.1.call-done = bf16[384,384]{1,0:T(8,128)(2,1)} async-done(((bf16[1536,384]{1,0:T(8,128)(2,1)}), bf16[384,384]{1,0:T(8,128)(2,1)}) %reduce-scatter.14.cloned.1.call-update) | async-done | bytes 294928 | tf_op jit(solution)/shard_map/reduce_scatter | solution.py:338
  460.4 39.5 %reduce-scatter.6.cloned.1.call-done = bf16[96,2304]{1,0:T(8,128)(2,1)} async-done(((bf16[384,2304]{1,0:T(8,128)(2,1)}), bf16[96,2304]{1,0:T(8,128)(2,1)}) %reduce-scatter.6.cloned.1.call-update) | async-done | bytes 442384 | tf_op jit(solution)/shard_map/reduce_scatter | solution.py:338
  503.3 17.0 %all-reduce.5 = (bf16[2304]{0:T(1024)(128)(2,1)S(1)}, bf16[1536]{0:T(1024)(128)(2,1)S(1)}) all-reduce(bf16[2304]{0:T(1024)(128)(2,1)S(1)} %add_convert_fusion.9, bf16[1536]{0:T(1024)(128)(2,1)S(1)} %add_convert_fusion.10), channel_id=3, replica_groups=mesh['section'=2,'group'=4,'rep'=4] {'group'}, use_global_device_ids=true, to_apply=%region_71.72.clone | all-reduce | flops 3840 | bytes 15360
  520.4 9.8 %all-reduce.3 = (bf16[1,576]{1,0:T(2,128)(2,1)S(1)}, bf16[1,384]{1,0:T(2,128)(2,1)S(1)}) all-reduce(bf16[1,576]{1,0:T(2,128)(2,1)S(1)} %broadcast_in_dim.142, bf16[1,384]{1,0:T(2,128)(2,1)S(1)} %broadcast_in_dim.172), channel_id=1, replica_groups=mesh['section'=2,'group'=4,'rep'=4] {'rep'}, use_global_device_ids=true, to_apply=%region_72.73 | all-reduce | flops 960 | bytes 3840 | tf_op jit(solution)/shard_map/psum | solution.py:340
  534.7 26.4 %all-reduce.8.cloned.1.call-done = (bf16[1,96,2304]{2,1,0:T(8,128)(2,1)}, bf16[1,96,1152]{2,1,0:T(8,128)(2,1)}, bf16[1,96,384]{2,1,0:T(8,128)(2,1)}, bf16[1,96,1536]{2,1,0:T(8,128)(2,1)}, bf16[1,384,384]{2,1,0:T(8,128)(2,1)}) async-done(((bf16[1,96,2304]{2,1,0:T(8,128)(2,1)}, bf16[1,96,1152]{2,1,0:T(8,128)(2,1)}, bf16[1,96,384]{2,1,0:T(8,128)(2,1)}, bf16[1,96,1536]{2,1,0:T(8,128)(2,1)}, ...) | async-done | bytes 1327120 | tf_op jit(solution)/shard_map/psum | solution.py:340
  562.7 2.0 broadcast_in_dim.141
  (501 shorter events, 96.0 us)
Async XLA Ops:
  7.2 123.4 %copy-start.64 = (bf16[2,256,384]{2,1,0:T(8,128)(2,1)S(1)}, bf16[2,256,384]{2,1,0:T(8,128)(2,1)}, u32[]{:S(2)}) copy-start(bf16[2,256,384]{2,1,0:T(8,128)(2,1)} %param.19) | copy-start | bytes 1179652
  7.2 34.4 %copy-start.114 = (bf16[1,96,384]{2,1,0:T(8,128)(2,1)S(1)}, bf16[1,96,384]{2,1,0:T(8,128)(2,1)}, u32[]{:S(2)}) copy-start(bf16[1,96,384]{2,1,0:T(8,128)(2,1)} %param.26) | copy-start | bytes 221188
  7.2 48.5 %copy-start.150 = (f32[2,384]{1,0:T(2,128)S(1)}, f32[2,384]{1,0:T(2,128)}, u32[]{:S(2)}) copy-start(f32[2,384]{1,0:T(2,128)} %param.20) | copy-start | bytes 9220
  7.2 50.3 %copy-start.102 = (bf16[1,96,1152]{2,1,0:T(8,128)(2,1)S(1)}, bf16[1,96,1152]{2,1,0:T(8,128)(2,1)}, u32[]{:S(2)}) copy-start(bf16[1,96,1152]{2,1,0:T(8,128)(2,1)} %param.25) | copy-start | bytes 663556
  7.2 81.6 %all-gather.6.cloned.1.call-start = ((), (), s32[]{:S(2)}) async-start(), calls=%async_computation.6 | async-start | bytes 1474560 | tf_op jit(solution)/shard_map/all_gather | solution.py:286
  8.0 80.9 %all-gather.8.cloned.1.call-start = ((), (), s32[]{:S(2)}) async-start(), calls=%async_computation.7 | async-start | bytes 1474560 | tf_op jit(solution)/shard_map/all_gather | solution.py:288
  8.7 121.8 %all-gather.4.cloned.1.call-start = ((), (), s32[]{:S(2)}) async-start(), calls=%async_computation.5 | async-start | bytes 2211840 | tf_op jit(solution)/shard_map/all_gather | solution.py:282
  9.4 371.7 %reduce-scatter.10.cloned.1.call-start = ((), (), s32[]{:S(2)}) async-start(), calls=%async_computation.10 | async-start | bytes 368640 | tf_op jit(solution)/shard_map/reduce_scatter | solution.py:338
  25.9 104.6 %copy-start.115 = (bf16[1536]{0:T(1024)(128)(2,1)}, bf16[1536]{0:T(1024)(128)(2,1)S(1)}, u32[]{:S(2)}) copy-start(bf16[1536]{0:T(1024)(128)(2,1)S(1)} %reduce.132) | copy-start | bytes 9220
  55.7 95.3 %copy-start.1 = (bf16[1,384,384]{2,1,0:T(8,128)(2,1)}, bf16[1,384,384]{2,1,0:T(8,128)(2,1)S(1)}, u32[]{:S(2)}) copy-start(bf16[1,384,384]{2,1,0:T(8,128)(2,1)S(1)} %all_gather.24) | copy-start | bytes 884740
  88.9 59.8 %copy-start.6 = (bf16[1,384,1152]{2,1,0:T(8,128)(2,1)}, bf16[1,384,1152]{2,1,0:T(8,128)(2,1)S(1)}, u32[]{:S(2)}) copy-start(bf16[1,384,1152]{2,1,0:T(8,128)(2,1)S(1)} %all_gather.23) | copy-start | bytes 2654212
  144.3 4.9 copy-start.25
  144.3 4.9 copy-start.36
  144.3 4.9 copy-start.103
  144.3 3.9 collective-permute-start
  155.3 2.3 collective-permute-start.1
  177.4 94.3 %copy-start.110 = (f32[2304]{0:T(1024)}, f32[2304]{0:T(1024)S(1)}, u32[]{:S(2)}) copy-start(f32[2304]{0:T(1024)S(1)} %get-tuple-element.381) | copy-start | bytes 27652
  177.4 94.3 %copy-start.127 = (f32[1536]{0:T(1024)}, f32[1536]{0:T(1024)S(1)}, u32[]{:S(2)}) copy-start(f32[1536]{0:T(1024)S(1)} %get-tuple-element.389) | copy-start | bytes 18436
  177.4 94.3 %collective-permute-start.2 = (bf16[1,256,384]{2,1,0:T(8,128)(2,1)S(1)}, bf16[1,256,384]{2,1,0:T(8,128)(2,1)S(1)}, u32[]{:S(2)}, u32[]{:S(2)}) collective-permute-start(bf16[1,256,384]{2,1,0:T(8,128)(2,1)S(1)} %get-tuple-element.363), channel_id=1, source_target_pairs={{16,0},{17,1},{18,2},{19,3},{20,4},{21,5},{22,6},{23,7},{24,8},{25... | collective-permute-start | bytes 589832 | tf_op jit(solution)/shard_map/ppermute | solution.py:20
  271.7 6.7 %copy-start.91 = (bf16[1,256,384]{2,1,0:T(8,128)(2,1)}, bf16[1,256,384]{2,1,0:T(8,128)(2,1)S(1)}, u32[]{:S(2)}) copy-start(bf16[1,256,384]{2,1,0:T(8,128)(2,1)S(1)} %collective-permute-done.2) | copy-start | bytes 589828
  271.7 4.7 copy-start.15
  271.7 4.7 copy-start.21
  289.2 5.4 copy-start.60
  289.2 5.4 copy-start.3
  289.2 5.4 copy-start.11
  289.2 5.3 copy-start.26
  289.2 5.3 copy-start.113
  290.4 3.3 collective-permute-start.3
  300.2 5.4 copy-start.166
  327.1 4.8 copy-start.178
  328.4 5.8 %copy-start.137 = (f32[1,384]{1,0:T(1,128)S(1)}, f32[1,384]{1,0:T(1,128)}, u32[]{:S(2)}) copy-start(f32[1,384]{1,0:T(1,128)} %get-tuple-element.282) | copy-start | bytes 4612 | tf_op jit(solution)/shard_map/cond
  328.4 5.8 %copy-start.172 = (f32[1,384]{1,0:T(1,128)S(1)}, f32[1,384]{1,0:T(1,128)}, u32[]{:S(2)}) copy-start(f32[1,384]{1,0:T(1,128)} %get-tuple-element.680) | copy-start | bytes 4612 | tf_op jit(solution)/shard_map/cond
  355.3 44.5 %reduce-scatter.8.cloned.1.call-start = ((), (), s32[]{:S(2)}) async-start(), calls=%async_computation.9 | async-start | bytes 1105920 | tf_op jit(solution)/shard_map/reduce_scatter | solution.py:338
  359.2 71.0 %reduce-scatter.12.cloned.1.call-start = ((), (), s32[]{:S(2)}) async-start(), calls=%async_computation.11 | async-start | bytes 1474560 | tf_op jit(solution)/shard_map/reduce_scatter | solution.py:338
  363.6 96.8 %reduce-scatter.14.cloned.1.call-start = ((), (), s32[]{:S(2)}) async-start(), calls=%async_computation.12 | async-start | bytes 1474560 | tf_op jit(solution)/shard_map/reduce_scatter | solution.py:338
  363.7 5.8 %copy-start.181 = (bf16[384]{0:T(512)(128)(2,1)S(1)}, bf16[384]{0:T(512)(128)(2,1)}, u32[]{:S(2)}) copy-start(bf16[384]{0:T(512)(128)(2,1)} %get-tuple-element.687) | copy-start | bytes 2308
  363.7 5.8 %copy-start.59 = (f32[256,384]{1,0:T(8,128)S(1)}, f32[256,384]{1,0:T(8,128)}, u32[]{:S(2)}) copy-start(f32[256,384]{1,0:T(8,128)} %copy-done.58) | copy-start | bytes 1179652
  369.4 130.5 %reduce-scatter.6.cloned.1.call-start = ((), (), s32[]{:S(2)}) async-start(), calls=%async_computation.8 | async-start | bytes 2211840 | tf_op jit(solution)/shard_map/reduce_scatter | solution.py:338
  376.7 123.2 %copy-start.149 = (f32[1,384]{1,0:T(1,128)S(1)}, f32[1,384]{1,0:T(1,128)}, u32[]{:S(2)}) copy-start(f32[1,384]{1,0:T(1,128)} %get-tuple-element.688) | copy-start | bytes 4612
  376.7 184.3 %all-reduce.8.cloned.1.call-start = ((), (), s32[]{:S(2)}) async-start(), calls=%async_computation.13 | async-start | bytes 2654208 | tf_op jit(solution)/shard_map/psum | solution.py:340
  378.9 152.5 %collective-permute-start.5 = (bf16[1,384]{1,0:T(2,128)(2,1)S(1)}, bf16[1,384]{1,0:T(2,128)(2,1)S(1)}, u32[]{:S(2)}, u32[]{:S(2)}) collective-permute-start(bf16[1,384]{1,0:T(2,128)(2,1)S(1)} %copy-done.183), channel_id=1, source_target_pairs={{16,0},{17,1},{18,2},{19,3},{20,4},{21,5},{22,6},{23,7},{24,8},{25... | collective-permute-start | bytes 2312 | tf_op jit(solution)/shard_map/ppermute | solution.py:20
  381.1 120.8 %copy-start.128 = (f32[1536]{0:T(1024)S(1)}, f32[1536]{0:T(1024)}, u32[]{:S(2)}) copy-start(f32[1536]{0:T(1024)} %copy-done.127) | copy-start | bytes 18436
  381.1 120.8 %copy-start.171 = (f32[1536]{0:T(1024)S(1)}, f32[1536]{0:T(1024)}, u32[]{:S(2)}) copy-start(f32[1536]{0:T(1024)} %get-tuple-element.772) | copy-start | bytes 18436
  499.9 31.5 %copy-start.173 = (f32[1,384]{1,0:T(1,128)S(1)}, f32[1,384]{1,0:T(1,128)}, u32[]{:S(2)}) copy-start(f32[1,384]{1,0:T(1,128)} %get-tuple-element.378) | copy-start | bytes 4612
  499.9 32.8 %copy-start.76 = (bf16[1,256,384]{2,1,0:T(8,128)(2,1)S(1)}, bf16[1,256,384]{2,1,0:T(8,128)(2,1)}, u32[]{:S(2)}) copy-start(bf16[1,256,384]{2,1,0:T(8,128)(2,1)} %copy-done.75) | copy-start | bytes 589828
  499.9 33.8 %copy-start.55 = (f32[1,256,384]{2,1,0:T(8,128)S(1)}, f32[1,256,384]{2,1,0:T(8,128)}, u32[]{:S(2)}) copy-start(f32[1,256,384]{2,1,0:T(8,128)} %get-tuple-element.748) | copy-start | bytes 1179652
  500.5 30.9 %collective-permute-start.4 = (bf16[1,384]{1,0:T(2,128)(2,1)S(1)}, bf16[1,384]{1,0:T(2,128)(2,1)S(1)}, u32[]{:S(2)}, u32[]{:S(2)}) collective-permute-start(bf16[1,384]{1,0:T(2,128)(2,1)S(1)} %get-tuple-element.770), channel_id=1, source_target_pairs={{16,0},{17,1},{18,2},{19,3},{20,4},{21,5},{22,6},{23,7},{24,8},{25... | collective-permute-start | bytes 2312 | tf_op jit(solution)/shard_map/ppermute | solution.py:20
  561.0 5.3 copy-start.99
  (121 other events, 286.0 us)
Sparse Core Ops, SparseCore 0:
  9.6 34.4 all-gather.5
  45.7 42.9 all-gather.7
  90.3 40.1 all-gather.3
  355.4 18.7 reduce-scatter.9
  376.9 22.8 reduce-scatter.7
  402.0 28.1 reduce-scatter.11
  432.5 27.8 reduce-scatter.13
  462.8 37.0 reduce-scatter.5
  504.0 57.0 all-reduce.7
where the time goes:
time: 584 us; the launch traced here: 574 us
  waiting for transfers between devices  284 us (49%)
  blocking collectives  97.2 us (17%)
  matrix products  60.4 us (10%)
  local copies, waits for them, and re-layouts  52.3 us (9%)
  other arithmetic  51.3 us (9%)
  between operations  18.8 us (3%)
  starting transfers between devices  8.63 us (1%)
    reduce_scatter x5, waiting for transfers between devices, body(): lax.psum_scatter(for_sending(totals), 'group', scatter_dimension=0, tiled...  119 us
    ppermute x6, waiting for transfers between devices, passed_along(): lax.ppermute(value, axis, [(source, source + steps) for source in range(f...  95.1 us
    all_gather x1, waiting for transfers between devices, body(): lax.all_gather(adaptive_weight, 'group', axis=1, tiled=True)  41.7 us
    all_gather x1, blocking collectives, body(): lax.all_gather(query_key_value_weight, 'group', axis=1, tiled=True)  31.4 us
    psum x1, waiting for transfers between devices, body(): lax.psum(for_sending(owned), 'rep')  26.4 us
    another operation x26, local copies, waits for them, and re-layouts  21.6 us
    unnamed x1, blocking collectives  17 us
    all_gather x1, blocking collectives, body(): lax.all_gather(output_projection_weight, 'group', axis=1, tiled=True)  14 us
  transfers between devices with their start and end apart: 15, of which 9 were waited for; matrix products, arithmetic and copies ran while one was open for 7% of the time, Pallas kernels for 0%

commit v1 on v0

--- a/solution.py
+++ b/solution.py
@@ -12,6 +12,23 @@
 MB = 2
 SLOTS = 1
 epsilon = 1e-06
+
+
+def in_order(blocks, dim):
+    blocks = jnp.moveaxis(blocks, 0, dim)
+    dims = blocks.shape
+    return blocks.reshape(*dims[:dim], dims[dim] * dims[dim + 1], *dims[dim + 2 :])
+
+
+def collect(value, axis, dim):
+    size = lax.axis_size(axis)
+    forward = [(i, (i + 1) % size) for i in range(size)]
+    blocks = [value]
+    while len(blocks) < size:
+        blocks.append(lax.ppermute(blocks[-1], axis, forward))
+    index = lax.axis_index(axis)
+    blocks = jnp.stack(blocks)[(index - jnp.arange(size)) % size]
+    return in_order(blocks, dim)
 
 
 def passed_along(value, axis, steps):
@@ -282,7 +299,7 @@
             lax.all_gather(adaptive_weight, "group", axis=1, tiled=True),
             lax.all_gather(adaptive_bias, "group", axis=1, tiled=True),
             lax.all_gather(query_key_value_weight, "group", axis=1, tiled=True),
-            lax.all_gather(output_projection_weight, "group", axis=1, tiled=True),
+            collect(output_projection_weight, "group", 1),
             lax.all_gather(first_dense_weight, "group", axis=1, tiled=True),
             lax.all_gather(first_dense_bias, "group", axis=1, tiled=True),
             lax.all_gather(second_dense_weight, "group", axis=1, tiled=True),

time: 584 us -> 584 us (level)
  blocking collectives: 97.2 us -> 82.2 us
  waiting for transfers between devices: 284 us -> 296 us
    ppermute x0 -> x3, waiting for transfers between devices: none -> 14.1 us  [collect(): blocks.append(lax.ppermute(blocks[-1], axis, forward))]
    all_gather x1 -> x0, blocking collectives: 14 us -> none  [body(): lax.all_gather(output_projection_weight, 'group', axis=1, tiled=True)]
  transfers between devices with their start and end apart: 15 -> 18, of which waited for: 9 -> 11; matrix products, arithmetic and copies ran while one was open for 7% -> 7% of each run, Pallas kernels for 0% -> 0%
where the time goes in v1:
time: 584 us; the launch traced here: 573 us
  waiting for transfers between devices  296 us (51%)
  blocking collectives  82.2 us (14%)
  matrix products  60.4 us (10%)
  other arithmetic  51.5 us (9%)
  local copies, waits for them, and re-layouts  51.4 us (9%)
  between operations  18.8 us (3%)
  starting transfers between devices  11.8 us (2%)
    reduce_scatter x5, waiting for transfers between devices, body(): lax.psum_scatter(for_sending(totals), 'group', scatter_dimension=0, tiled...  119 us
    ppermute x6, waiting for transfers between devices, passed_along(): lax.ppermute(value, axis, [(source, source + steps) for source in range(f...  95.1 us
    all_gather x1, waiting for transfers between devices, body(): lax.all_gather(adaptive_weight, 'group', axis=1, tiled=True)  39.3 us
    all_gather x1, blocking collectives, body(): lax.all_gather(query_key_value_weight, 'group', axis=1, tiled=True)  32.5 us
    psum x1, waiting for transfers between devices, body(): lax.psum(for_sending(owned), 'rep')  26.3 us
    another operation x26, local copies, waits for them, and re-layouts  21.6 us
    unnamed x1, blocking collectives  17 us
    ppermute x3, waiting for transfers between devices, collect(): blocks.append(lax.ppermute(blocks[-1], axis, forward))  14.1 us
  transfers between devices with their start and end apart: 18, of which 11 were waited for; matrix products, arithmetic and copies ran while one was open for 7% of the time, Pallas kernels for 0%

profile of v1, /device:TPU:0, one launch (start us, length us, event | category | flops | bytes accessed | tf_op | source)
XLA Modules:
  0.0 573.1 jit_solution(1915244248838444284)
XLA Ops:
  9.5 3.1 collective-permute-start
  13.2 1.9 convert_reduce_fusion.10
  16.5 32.5 %all_gather.20 = bf16[1,384,1152]{2,1,0:T(8,128)(2,1)S(1)} all-gather(bf16[1,96,1152]{2,1,0:T(8,128)(2,1)} %param.25), channel_id=1, replica_groups=mesh['section'=2,'group'=4,'rep'=4] {'group'}, dimensions={1}, use_global_device_ids=true | all-gather | bytes 1105920 | tf_op jit(solution)/shard_map/all_gather | solution.py:301
  50.4 11.9 %all_gather.22 = bf16[1,1536]{1,0:T(2,128)(2,1)S(1)} all-gather(bf16[1,384]{1,0:T(2,128)(2,1)S(1)} %copy-done.182), channel_id=1, replica_groups=mesh['section'=2,'group'=4,'rep'=4] {'group'}, dimensions={1}, use_global_device_ids=true | all-gather | bytes 3840 | tf_op jit(solution)/shard_map/all_gather | solution.py:304
  65.1 11.0 %all-reduce = bf16[2304]{0:T(1024)(128)(2,1)S(1)} all-reduce(bf16[2304]{0:T(1024)(128)(2,1)S(1)} %dynamic-update-slice), channel_id=1, replica_groups=mesh['section'=2,'group'=4,'rep'=4] {'group'}, use_global_device_ids=true, to_apply=%add | all-reduce | flops 2304 | bytes 9216 | tf_op jit(solution)/shard_map/squeeze | solution.py:274
  76.2 7.7 %collective-permute-done.1 = bf16[1,96,384]{2,1,0:T(8,128)(2,1)S(1)} collective-permute-done((bf16[1,96,384]{2,1,0:T(8,128)(2,1)S(1)}, bf16[1,96,384]{2,1,0:T(8,128)(2,1)S(1)}, u32[]{:S(2)}, u32[]{:S(2)}) %collective-permute-start.1) | collective-permute-done | bytes 73760 | tf_op jit(solution)/shard_map/ppermute | solution.py:28
  84.0 6.4 %collective-permute-done.2 = bf16[1,96,384]{2,1,0:T(8,128)(2,1)S(1)} collective-permute-done((bf16[1,96,384]{2,1,0:T(8,128)(2,1)S(1)}, bf16[1,96,384]{2,1,0:T(8,128)(2,1)S(1)}, u32[]{:S(2)}, u32[]{:S(2)}) %collective-permute-start.2) | collective-permute-done | bytes 73760 | tf_op jit(solution)/shard_map/ppermute | solution.py:28
  91.1 39.3 %all-gather.4.cloned.1.call-done = bf16[1,384,2304]{2,1,0:T(8,128)(2,1)} async-done(((bf16[1,96,2304]{2,1,0:T(8,128)(2,1)}), bf16[1,384,2304]{2,1,0:T(8,128)(2,1)}) %all-gather.4.cloned.1.call-update) | async-done | bytes 1769488 | tf_op jit(solution)/shard_map/all_gather | solution.py:299
  130.4 13.2 %conditional.4 = (bf16[1,256,384]{2,1,0:T(8,128)(2,1)S(1)}, f32[1,384]{1,0:T(1,128)}, f32[1,2304]{1,0:T(1,128)S(1)}, bf16[1,256,384]{2,1,0:T(8,128)(2,1)}, bf16[...) conditional(s32[]{:T(128)} %convert_element_type.491, () %tuple.65, ...), branch_computations={%region_0.1_spmd, %region_1.8_spmd} | conditional | flops 1021386368 | bytes 41346496 | solution.py:317
  130.4 1.8 convolution_reduce_fusion
  138.8 2.8 fusion.16
  141.6 1.9 fusion.29
  145.1 1.8 convolution_reduce_fusion.2
  156.9 10.2 %conditional.5 = (bf16[1,256,384]{2,1,0:T(8,128)(2,1)S(1)}, f32[1,384]{1,0:T(1,128)}, f32[1,2304]{1,0:T(1,128)}, bf16[1,256,384]{2,1,0:T(8,128)(2,1)}, bf16[1,25...) conditional(s32[]{:T(128)} %convert_element_type.509, () %tuple.67, ...), branch_computations={%region_14.15_spmd, %region_15.22_spmd} | conditional | flops 1021386368 | bytes 41874824 | solution.py:317
  167.1 9.5 %conditional.6 = (f32[384,2304]{1,0:T(8,128)}, f32[2304]{0:T(1024)S(1)}, f32[1536]{0:T(1024)S(1)}, bf16[1,256,384]{2,1,0:T(8,128)(2,1)S(1)}, bf16[1,384]{1,0:T(2...) conditional(s32[]{:T(128)} %convert_element_type.509, () %tuple.70, ...), branch_computations={%region_22.23_spmd, %region_23.40_spmd} | conditional | flops 2089162752 | bytes 87958680 | solution.py:340
  174.6 2.0 broadcast.961
  178.1 92.8 %collective-permute-done.5 = bf16[1,256,384]{2,1,0:T(8,128)(2,1)S(1)} collective-permute-done((bf16[1,256,384]{2,1,0:T(8,128)(2,1)S(1)}, bf16[1,256,384]{2,1,0:T(8,128)(2,1)S(1)}, u32[]{:S(2)}, u32[]{:S(2)}) %collective-permute-start.5) | collective-permute-done | bytes 196640 | tf_op jit(solution)/shard_map/ppermute | solution.py:37
  271.0 4.6 convert_reduce_fusion.8
  277.6 2.1 fusion.169
  290.9 2.0 collective-permute-done.6
  293.8 58.3 %conditional.7 = (f32[1,256,384]{2,1,0:T(8,128)}, f32[1,384]{1,0:T(1,128)}, f32[384,2304]{1,0:T(8,128)}, f32[2304]{0:T(1024)}, f32[1536]{0:T(1024)}, /*index=5*/...) conditional(s32[]{:T(128)} %convert_element_type.491, () %tuple.69, ...), branch_computations={%region_45.46_spmd, %region_46.63_spmd} | conditional | flops 2088473856 | bytes 92844544 | solution.py:340
  297.5 2.0 convert_reduce_fusion.7
  299.4 1.8 multiply_reduce_fusion.7
  301.3 3.6 convert_reduce_fusion.5
  310.5 1.9 multiply_reduce_fusion.8
  316.5 2.1 convolution_bitcast_fusion.9
  318.6 2.1 copy.164
  320.7 2.1 copy.131
  331.4 2.0 add_add_fusion.5
  335.7 1.9 copy.162
  337.6 3.3 convolution_bitcast_fusion.5
  340.9 3.2 copy.168
  344.1 2.0 convolution_bitcast_fusion.6
  346.1 3.2 copy.166
  349.3 2.9 broadcast_multiply_fusion.7
  352.1 2.3 add_convert_fusion.7
  354.6 3.7 add_convert_fusion.6
  358.7 4.1 add_convert_fusion.5
  362.9 5.7 add_convert_fusion.4
  371.0 4.9 add_convert_fusion.3
  380.3 18.7 %reduce-scatter.8.cloned.1.call-done = bf16[96,1152]{1,0:T(8,128)(2,1)} async-done(((bf16[384,1152]{1,0:T(8,128)(2,1)}), bf16[96,1152]{1,0:T(8,128)(2,1)}) %reduce-scatter.8.cloned.1.call-update) | async-done | bytes 221200 | tf_op jit(solution)/shard_map/reduce_scatter | solution.py:355
  399.0 30.4 %reduce-scatter.12.cloned.1.call-done = bf16[96,1536]{1,0:T(8,128)(2,1)} async-done(((bf16[384,1536]{1,0:T(8,128)(2,1)}), bf16[96,1536]{1,0:T(8,128)(2,1)}) %reduce-scatter.12.cloned.1.call-update) | async-done | bytes 294928 | tf_op jit(solution)/shard_map/reduce_scatter | solution.py:355
  429.5 30.2 %reduce-scatter.14.cloned.1.call-done = bf16[384,384]{1,0:T(8,128)(2,1)} async-done(((bf16[1536,384]{1,0:T(8,128)(2,1)}), bf16[384,384]{1,0:T(8,128)(2,1)}) %reduce-scatter.14.cloned.1.call-update) | async-done | bytes 294928 | tf_op jit(solution)/shard_map/reduce_scatter | solution.py:355
  459.7 39.5 %reduce-scatter.6.cloned.1.call-done = bf16[96,2304]{1,0:T(8,128)(2,1)} async-done(((bf16[384,2304]{1,0:T(8,128)(2,1)}), bf16[96,2304]{1,0:T(8,128)(2,1)}) %reduce-scatter.6.cloned.1.call-update) | async-done | bytes 442384 | tf_op jit(solution)/shard_map/reduce_scatter | solution.py:355
  502.5 17.0 %all-reduce.5 = (bf16[2304]{0:T(1024)(128)(2,1)S(1)}, bf16[1536]{0:T(1024)(128)(2,1)S(1)}) all-reduce(bf16[2304]{0:T(1024)(128)(2,1)S(1)} %add_convert_fusion.9, bf16[1536]{0:T(1024)(128)(2,1)S(1)} %add_convert_fusion.10), channel_id=3, replica_groups=mesh['section'=2,'group'=4,'rep'=4] {'group'}, use_global_device_ids=true, to_apply=%region_71.72.clone | all-reduce | flops 3840 | bytes 15360
  519.7 9.8 %all-reduce.3 = (bf16[1,576]{1,0:T(2,128)(2,1)S(1)}, bf16[1,384]{1,0:T(2,128)(2,1)S(1)}) all-reduce(bf16[1,576]{1,0:T(2,128)(2,1)S(1)} %broadcast_in_dim.142, bf16[1,384]{1,0:T(2,128)(2,1)S(1)} %broadcast_in_dim.150), channel_id=1, replica_groups=mesh['section'=2,'group'=4,'rep'=4] {'rep'}, use_global_device_ids=true, to_apply=%region_72.73 | all-reduce | flops 960 | bytes 3840 | tf_op jit(solution)/shard_map/psum | solution.py:357
  533.9 26.3 %all-reduce.8.cloned.1.call-done = (bf16[1,96,2304]{2,1,0:T(8,128)(2,1)}, bf16[1,96,1152]{2,1,0:T(8,128)(2,1)}, bf16[1,96,384]{2,1,0:T(8,128)(2,1)}, bf16[1,96,1536]{2,1,0:T(8,128)(2,1)}, bf16[1,384,384]{2,1,0:T(8,128)(2,1)}) async-done(((bf16[1,96,2304]{2,1,0:T(8,128)(2,1)}, bf16[1,96,1152]{2,1,0:T(8,128)(2,1)}, bf16[1,96,384]{2,1,0:T(8,128)(2,1)}, bf16[1,96,1536]{2,1,0:T(8,128)(2,1)}, ...) | async-done | bytes 1327120 | tf_op jit(solution)/shard_map/psum | solution.py:357
  561.9 2.0 broadcast_in_dim.141
  (508 shorter events, 98.6 us)
Async XLA Ops:
  7.2 56.4 %copy-start.179 = (u32[32]{0:T(128)S(1)}, u32[32]{0:T(128)}, u32[]{:S(2)}) copy-start(u32[32]{0:T(128)} %constant.323) | copy-start | bytes 388
  7.2 83.2 %copy-start.111 = (bf16[1,96,384]{2,1,0:T(8,128)(2,1)S(1)}, bf16[1,96,384]{2,1,0:T(8,128)(2,1)}, u32[]{:S(2)}) copy-start(bf16[1,96,384]{2,1,0:T(8,128)(2,1)} %param.26) | copy-start | bytes 221188
  7.2 43.1 %copy-start.178 = (bf16[1,576]{1,0:T(2,128)(2,1)S(1)}, bf16[1,576]{1,0:T(2,128)(2,1)}, u32[]{:S(2)}) copy-start(bf16[1,576]{1,0:T(2,128)(2,1)} %param.24) | copy-start | bytes 3460
  7.2 43.1 %copy-start.182 = (bf16[1,384]{1,0:T(2,128)(2,1)S(1)}, bf16[1,384]{1,0:T(2,128)(2,1)}, u32[]{:S(2)}) copy-start(bf16[1,384]{1,0:T(2,128)(2,1)} %param.28) | copy-start | bytes 2308
  7.2 55.6 %copy-start.64 = (bf16[2,256,384]{2,1,0:T(8,128)(2,1)S(1)}, bf16[2,256,384]{2,1,0:T(8,128)(2,1)}, u32[]{:S(2)}) copy-start(bf16[2,256,384]{2,1,0:T(8,128)(2,1)} %param.19) | copy-start | bytes 1179652
  7.2 83.8 %all-gather.6.cloned.1.call-start = ((), (), s32[]{:S(2)}) async-start(), calls=%async_computation.6 | async-start | bytes 1474560 | tf_op jit(solution)/shard_map/all_gather | solution.py:303
  8.0 83.1 %all-gather.8.cloned.1.call-start = ((), (), s32[]{:S(2)}) async-start(), calls=%async_computation.7 | async-start | bytes 1474560 | tf_op jit(solution)/shard_map/all_gather | solution.py:305
  8.7 121.7 %all-gather.4.cloned.1.call-start = ((), (), s32[]{:S(2)}) async-start(), calls=%async_computation.5 | async-start | bytes 2211840 | tf_op jit(solution)/shard_map/all_gather | solution.py:299
  9.5 370.8 %reduce-scatter.10.cloned.1.call-start = ((), (), s32[]{:S(2)}) async-start(), calls=%async_computation.10 | async-start | bytes 368640 | tf_op jit(solution)/shard_map/reduce_scatter | solution.py:355
  9.5 66.7 %collective-permute-start = (bf16[1,96,384]{2,1,0:T(8,128)(2,1)}, bf16[1,96,384]{2,1,0:T(8,128)(2,1)S(1)}, u32[]{:S(2)}, u32[]{:S(2)}) collective-permute-start(bf16[1,96,384]{2,1,0:T(8,128)(2,1)} %param.26), channel_id=1, source_target_pairs={{0,4},{4,8},{8,12},{12,0},{1,5},{5,9},{9,13},{13,1},{2,6},{6,10},{... | collective-permute-start | bytes 221192 | tf_op jit(solution)/shard_map/ppermute | solution.py:28
  49.0 99.0 %copy-start.6 = (bf16[1,384,1152]{2,1,0:T(8,128)(2,1)}, bf16[1,384,1152]{2,1,0:T(8,128)(2,1)S(1)}, u32[]{:S(2)}) copy-start(bf16[1,384,1152]{2,1,0:T(8,128)(2,1)S(1)} %all_gather.20) | copy-start | bytes 2654212
  62.3 68.2 %copy-start.112 = (bf16[1536]{0:T(1024)(128)(2,1)}, bf16[1536]{0:T(1024)(128)(2,1)S(1)}, u32[]{:S(2)}) copy-start(bf16[1536]{0:T(1024)(128)(2,1)S(1)} %reduce.132) | copy-start | bytes 9220
  76.2 7.8 %collective-permute-start.1 = (bf16[1,96,384]{2,1,0:T(8,128)(2,1)S(1)}, bf16[1,96,384]{2,1,0:T(8,128)(2,1)S(1)}, u32[]{:S(2)}, u32[]{:S(2)}) collective-permute-start(bf16[1,96,384]{2,1,0:T(8,128)(2,1)S(1)} %collective-permute-done), channel_id=1, source_target_pairs={{0,4},{4,8},{8,12},{12,0},{1,5},{5,9},{9,13},{13,1},{2,6},{6,10},{... | collective-permute-start | bytes 221192 | tf_op jit(solution)/shard_map/ppermute | solution.py:28
  84.0 6.4 %collective-permute-start.2 = (bf16[1,96,384]{2,1,0:T(8,128)(2,1)S(1)}, bf16[1,96,384]{2,1,0:T(8,128)(2,1)S(1)}, u32[]{:S(2)}, u32[]{:S(2)}) collective-permute-start(bf16[1,96,384]{2,1,0:T(8,128)(2,1)S(1)} %collective-permute-done.1), channel_id=1, source_target_pairs={{0,4},{4,8},{8,12},{12,0},{1,5},{5,9},{9,13},{13,1},{2,6},{6,10},{... | collective-permute-start | bytes 221192 | tf_op jit(solution)/shard_map/ppermute | solution.py:28
  91.0 59.3 %copy-start.1 = (bf16[4,96,384]{2,1,0:T(8,128)(2,1)}, bf16[4,96,384]{2,1,0:T(8,128)(2,1)S(1)}, u32[]{:S(2)}) copy-start(bf16[4,96,384]{2,1,0:T(8,128)(2,1)S(1)} %gather_fusion) | copy-start | bytes 884740
  143.6 5.0 copy-start.25
  143.6 5.0 copy-start.36
  143.6 4.0 collective-permute-start.3
  154.5 2.3 collective-permute-start.4
  176.6 94.3 %copy-start.107 = (f32[2304]{0:T(1024)}, f32[2304]{0:T(1024)S(1)}, u32[]{:S(2)}) copy-start(f32[2304]{0:T(1024)S(1)} %get-tuple-element.381) | copy-start | bytes 27652
  176.6 94.3 %copy-start.124 = (f32[1536]{0:T(1024)}, f32[1536]{0:T(1024)S(1)}, u32[]{:S(2)}) copy-start(f32[1536]{0:T(1024)S(1)} %get-tuple-element.389) | copy-start | bytes 18436
  176.6 94.3 %collective-permute-start.5 = (bf16[1,256,384]{2,1,0:T(8,128)(2,1)S(1)}, bf16[1,256,384]{2,1,0:T(8,128)(2,1)S(1)}, u32[]{:S(2)}, u32[]{:S(2)}) collective-permute-start(bf16[1,256,384]{2,1,0:T(8,128)(2,1)S(1)} %get-tuple-element.363), channel_id=1, source_target_pairs={{16,0},{17,1},{18,2},{19,3},{20,4},{21,5},{22,6},{23,7},{24,8},{25... | collective-permute-start | bytes 589832 | tf_op jit(solution)/shard_map/ppermute | solution.py:37
  270.9 6.7 %copy-start.91 = (bf16[1,256,384]{2,1,0:T(8,128)(2,1)}, bf16[1,256,384]{2,1,0:T(8,128)(2,1)S(1)}, u32[]{:S(2)}) copy-start(bf16[1,256,384]{2,1,0:T(8,128)(2,1)S(1)} %collective-permute-done.5) | copy-start | bytes 589828
  288.4 5.4 copy-start.60
  288.4 5.4 copy-start.3
  288.4 5.4 copy-start.11
  288.4 5.3 copy-start.26
  288.5 5.3 copy-start.110
  289.6 3.3 collective-permute-start.6
  299.4 5.4 copy-start.162
  327.6 5.8 %copy-start.134 = (f32[1,384]{1,0:T(1,128)S(1)}, f32[1,384]{1,0:T(1,128)}, u32[]{:S(2)}) copy-start(f32[1,384]{1,0:T(1,128)} %get-tuple-element.282) | copy-start | bytes 4612 | tf_op jit(solution)/shard_map/cond
  327.6 5.8 %copy-start.168 = (f32[1,384]{1,0:T(1,128)S(1)}, f32[1,384]{1,0:T(1,128)}, u32[]{:S(2)}) copy-start(f32[1,384]{1,0:T(1,128)} %get-tuple-element.680) | copy-start | bytes 4612 | tf_op jit(solution)/shard_map/cond
  354.5 44.5 %reduce-scatter.8.cloned.1.call-start = ((), (), s32[]{:S(2)}) async-start(), calls=%async_computation.9 | async-start | bytes 1105920 | tf_op jit(solution)/shard_map/reduce_scatter | solution.py:355
  358.4 71.1 %reduce-scatter.12.cloned.1.call-start = ((), (), s32[]{:S(2)}) async-start(), calls=%async_computation.11 | async-start | bytes 1474560 | tf_op jit(solution)/shard_map/reduce_scatter | solution.py:355
  362.8 96.9 %reduce-scatter.14.cloned.1.call-start = ((), (), s32[]{:S(2)}) async-start(), calls=%async_computation.12 | async-start | bytes 1474560 | tf_op jit(solution)/shard_map/reduce_scatter | solution.py:355
  362.9 5.8 %copy-start.177 = (bf16[384]{0:T(512)(128)(2,1)S(1)}, bf16[384]{0:T(512)(128)(2,1)}, u32[]{:S(2)}) copy-start(bf16[384]{0:T(512)(128)(2,1)} %get-tuple-element.687) | copy-start | bytes 2308
  362.9 5.8 %copy-start.59 = (f32[256,384]{1,0:T(8,128)S(1)}, f32[256,384]{1,0:T(8,128)}, u32[]{:S(2)}) copy-start(f32[256,384]{1,0:T(8,128)} %copy-done.58) | copy-start | bytes 1179652
  368.6 130.5 %reduce-scatter.6.cloned.1.call-start = ((), (), s32[]{:S(2)}) async-start(), calls=%async_computation.8 | async-start | bytes 2211840 | tf_op jit(solution)/shard_map/reduce_scatter | solution.py:355
  375.9 123.3 %copy-start.146 = (f32[1,384]{1,0:T(1,128)S(1)}, f32[1,384]{1,0:T(1,128)}, u32[]{:S(2)}) copy-start(f32[1,384]{1,0:T(1,128)} %get-tuple-element.688) | copy-start | bytes 4612
  375.9 184.4 %all-reduce.8.cloned.1.call-start = ((), (), s32[]{:S(2)}) async-start(), calls=%async_computation.13 | async-start | bytes 2654208 | tf_op jit(solution)/shard_map/psum | solution.py:357
  378.1 152.6 %collective-permute-start.8 = (bf16[1,384]{1,0:T(2,128)(2,1)S(1)}, bf16[1,384]{1,0:T(2,128)(2,1)S(1)}, u32[]{:S(2)}, u32[]{:S(2)}) collective-permute-start(bf16[1,384]{1,0:T(2,128)(2,1)S(1)} %copy-done.181), channel_id=1, source_target_pairs={{16,0},{17,1},{18,2},{19,3},{20,4},{21,5},{22,6},{23,7},{24,8},{25... | collective-permute-start | bytes 2312 | tf_op jit(solution)/shard_map/ppermute | solution.py:37
  380.3 120.8 %copy-start.125 = (f32[1536]{0:T(1024)S(1)}, f32[1536]{0:T(1024)}, u32[]{:S(2)}) copy-start(f32[1536]{0:T(1024)} %copy-done.124) | copy-start | bytes 18436
  380.3 120.8 %copy-start.167 = (f32[1536]{0:T(1024)S(1)}, f32[1536]{0:T(1024)}, u32[]{:S(2)}) copy-start(f32[1536]{0:T(1024)} %get-tuple-element.772) | copy-start | bytes 18436
  499.1 31.5 %copy-start.169 = (f32[1,384]{1,0:T(1,128)S(1)}, f32[1,384]{1,0:T(1,128)}, u32[]{:S(2)}) copy-start(f32[1,384]{1,0:T(1,128)} %get-tuple-element.378) | copy-start | bytes 4612
  499.2 32.8 %copy-start.76 = (bf16[1,256,384]{2,1,0:T(8,128)(2,1)S(1)}, bf16[1,256,384]{2,1,0:T(8,128)(2,1)}, u32[]{:S(2)}) copy-start(bf16[1,256,384]{2,1,0:T(8,128)(2,1)} %copy-done.75) | copy-start | bytes 589828
  499.2 33.8 %copy-start.55 = (f32[1,256,384]{2,1,0:T(8,128)S(1)}, f32[1,256,384]{2,1,0:T(8,128)}, u32[]{:S(2)}) copy-start(f32[1,256,384]{2,1,0:T(8,128)} %get-tuple-element.748) | copy-start | bytes 1179652
  499.8 30.9 %collective-permute-start.7 = (bf16[1,384]{1,0:T(2,128)(2,1)S(1)}, bf16[1,384]{1,0:T(2,128)(2,1)S(1)}, u32[]{:S(2)}, u32[]{:S(2)}) collective-permute-start(bf16[1,384]{1,0:T(2,128)(2,1)S(1)} %get-tuple-element.770), channel_id=1, source_target_pairs={{16,0},{17,1},{18,2},{19,3},{20,4},{21,5},{22,6},{23,7},{24,8},{25... | collective-permute-start | bytes 2312 | tf_op jit(solution)/shard_map/ppermute | solution.py:37
  560.3 5.3 copy-start.99
  (123 other events, 296.4 us)
Sparse Core Ops, SparseCore 0:
  9.6 44.5 all-gather.5
  55.8 33.1 all-gather.7
  90.6 39.7 all-gather.3
  354.6 18.7 reduce-scatter.9
  376.2 22.8 reduce-scatter.7
  401.2 28.2 reduce-scatter.11
  431.8 27.8 reduce-scatter.13
  462.0 37.0 reduce-scatter.5
  503.2 57.0 all-reduce.7
